TPU v7x, 32 devices: a whole 2x2x4 slice. The times are simulated.
32 devices in a mesh: wide: 8 (over z, y), narrow: 4 (over x, core).
Axes of the slice: x: 2, y: 2, z: 4, core: 2. Of those that a mesh axis runs over, the one named last changes fastest.
Arguments:
- amplitudes: bfloat16 [3072, 8192], P(None, ('wide', 'narrow')), may hold values from -6 to 6
- integrals: bfloat16 [8192, 4096], P('wide', 'narrow'), may hold values from -0.0625 to 0.0625
- old_residual: float32 [3072, 4096], P('wide', 'narrow'), may hold values from -6 to 6
Outputs:
- new_residual: float32 [3072, 4096], P('wide', 'narrow')
All inputs are finite; a program needn't handle non-finite values.
Results may differ from a plain program's by a relative error of at most 0.0003.
Values may be sent and summed in bfloat16 or wider, within the bound.
A program may use at most 128 MiB of HBM per device.

v0:
```python
import jax
import jax.numpy as jnp
from jax import lax
from jax.sharding import PartitionSpec as P


def broadcast(value, axis, source):
    kept = jnp.where(lax.axis_index(axis) == source, value, 0).astype(value.dtype)
    return lax.psum(kept, axis)


def per_device(amplitudes, integrals, old_residual):
    panels = lax.axis_size("narrow")
    sub_rows = integrals.shape[0] // panels
    stacked = integrals.reshape(panels, sub_rows, integrals.shape[1])
    total = old_residual
    row_amps = lax.all_to_all(amplitudes, "wide", split_axis=0, concat_axis=1, tiled=True)
    for column in range(panels):
        panel = broadcast(row_amps, "narrow", column)
        panel_ints = lax.all_gather(stacked[column], "wide", axis=0, tiled=True)
        total = total + jnp.dot(panel, panel_ints, preferred_element_type=jnp.float32)
    return total


def solution(mesh):
    placed = (P(None, ("wide", "narrow")), P("wide", "narrow"), P("wide", "narrow"))
    return jax.shard_map(
        per_device, mesh=mesh, in_specs=placed, out_specs=P("wide", "narrow"), check_vma=False
    )
```

profile of v0, /device:TPU:0, one launch (start us, length us, event | category | flops | bytes accessed | tf_op | source)
XLA Modules:
  0.0 372.1 jit_solution(5571402939716150730)
XLA Ops:
  7.4 7.3 %all-to-all-start = ((bf16[8,384,256]{2,1,0:T(8,128)(2,1)}), bf16[8,384,256]{2,1,0:T(8,128)(2,1)S(1)}, u32[]{:S(2)}, u32[]{:S(2)}) async-start(bf16[8,384,256]{2,1,0:T(8,128)(2,1)} %bitcast.25), calls=%async_computation | async-start | bytes 3145728 | tf_op jit(solution)/shard_map/all_to_all | solution.py:17
  14.7 36.9 %all-to-all-done = bf16[8,384,256]{2,1,0:T(8,128)(2,1)S(1)} async-done(((bf16[8,384,256]{2,1,0:T(8,128)(2,1)}), bf16[8,384,256]{2,1,0:T(8,128)(2,1)S(1)}, u32[]{:S(2)}, u32[]{:S(2)}) %all-to-all-start) | async-done | bytes 1572896 | tf_op jit(solution)/shard_map/all_to_all | solution.py:17
  51.7 2.3 select_bitcast_fusion
  53.9 2.6 copy.4
  56.5 2.8 copy.5
  59.3 1.6 copy.6
  60.8 1.6 copy.7
  62.4 0.0 all-gather.5.cloned.1.call-start
  62.5 1.5 copy-done.2
  64.0 1.4 fusion
  65.5 0.0 all-gather.7.cloned.1.call-start
  65.5 0.5 all-gather.7.cloned.1.call-update
  66.1 0.0 all-gather.9.cloned.1.call-start
  66.1 0.5 all-gather.9.cloned.1.call-update
  66.6 0.0 all-gather.11.cloned.1.call-start
  66.7 0.7 all-gather.11.cloned.1.call-update
  67.4 114.5 %all-reduce.3.cloned.1.call-done = (bf16[384,2048]{0,1:T(8,128)(2,1)}, bf16[384,2048]{0,1:T(8,128)(2,1)}, bf16[384,2048]{0,1:T(8,128)(2,1)}, bf16[384,2048]{0,1:T(8,128)(2,1)}) async-done(((bf16[384,2048]{0,1:T(8,128)(2,1)}, bf16[384,2048]{0,1:T(8,128)(2,1)}, bf16[384,2048]{0,1:T(8,128)(2,1)}, bf16[384,2048]{0,1:T(8,128)(2,1)}), (bf16[384,2048]{0,1:T(8,128)(2,1)}, bf16[384,2048]{0,1:T(8,128)(2,1)}, ...) | async-done | bytes 6291472 | tf_op jit(solution)/shard_map/psum | solution.py:9
  181.8 5.7 %fusion.1 = f32[384,1024]{1,0:T(8,128)} fusion(bf16[384,2048]{0,1:T(8,128)(2,1)} %get-tuple-element.7, bf16[2048,1024]{1,0:T(8,128)(2,1)} %all-gather.5.cloned.1.call-done), kind=kOutput, calls=%fused_computation.6 | convolution fusion | flops 1610612736 | bytes 7340032 | tf_op jit(solution)/shard_map/dot_general | solution.py:21
  187.6 23.4 %all-gather.7.cloned.1.call-done = bf16[2048,1024]{1,0:T(8,128)(2,1)} async-done(((bf16[256,1024]{1,0:T(8,128)(2,1)}), bf16[2048,1024]{1,0:T(8,128)(2,1)}) %all-gather.7.cloned.1.call-update) | async-done | bytes 4194320 | tf_op jit(solution)/shard_map/all_gather | solution.py:20
  211.0 5.2 %fusion.2 = f32[384,1024]{1,0:T(8,128)} fusion(bf16[384,2048]{0,1:T(8,128)(2,1)S(1)} %copy-done.4, bf16[2048,1024]{1,0:T(8,128)(2,1)} %all-gather.7.cloned.1.call-done), kind=kOutput, calls=%fused_computation.7 | convolution fusion | flops 1610612736 | bytes 7340032 | tf_op jit(solution)/shard_map/dot_general | solution.py:21
  216.1 68.2 %all-gather.9.cloned.1.call-done = bf16[2048,1024]{1,0:T(8,128)(2,1)} async-done(((bf16[256,1024]{1,0:T(8,128)(2,1)}), bf16[2048,1024]{1,0:T(8,128)(2,1)}) %all-gather.9.cloned.1.call-update) | async-done | bytes 4194320 | tf_op jit(solution)/shard_map/all_gather | solution.py:20
  284.4 5.8 %fusion.3 = f32[384,1024]{1,0:T(8,128)} fusion(bf16[384,2048]{0,1:T(8,128)(2,1)} %get-tuple-element.5, bf16[2048,1024]{1,0:T(8,128)(2,1)} %all-gather.9.cloned.1.call-done), kind=kOutput, calls=%fused_computation.8 | convolution fusion | flops 1610612736 | bytes 7340032 | tf_op jit(solution)/shard_map/dot_general | solution.py:21
  290.1 67.8 %all-gather.11.cloned.1.call-done = bf16[2048,1024]{1,0:T(8,128)(2,1)} async-done(((bf16[256,1024]{1,0:T(8,128)(2,1)}), bf16[2048,1024]{1,0:T(8,128)(2,1)}) %all-gather.11.cloned.1.call-update) | async-done | bytes 4194320 | tf_op jit(solution)/shard_map/all_gather | solution.py:20
  357.9 6.6 %add_add_fusion = f32[384,1024]{1,0:T(8,128)} fusion(f32[384,1024]{1,0:T(8,128)} %fusion.3, f32[384,1024]{1,0:T(8,128)} %fusion.2, f32[384,1024]{1,0:T(8,128)S(1)} %copy-done.3, f32[384,1024]{1,0:T(8,128)} %fusion.1, bf16[384,2048]{0,1:T(8,128)(2,1)S(1)} %copy-done.1, bf16[2048,1024]{1,0:T(8,128)(2,1)} %all-gather.11.cloned.1.call-done), kind=kOutput, calls=%fused_computation.1 | convolution fusion | flops 1612185600 | bytes 13631488 | tf_op jit(solution)/shard_map/dot_general | solution.py:21
  (13 shorter events, 0.1 us)
Async XLA Ops:
  7.4 44.3 %all-to-all-start = ((bf16[8,384,256]{2,1,0:T(8,128)(2,1)}), bf16[8,384,256]{2,1,0:T(8,128)(2,1)S(1)}, u32[]{:S(2)}, u32[]{:S(2)}) async-start(bf16[8,384,256]{2,1,0:T(8,128)(2,1)} %bitcast.25), calls=%async_computation | async-start | bytes 3145728 | tf_op jit(solution)/shard_map/all_to_all | solution.py:17
  14.6 167.2 %all-reduce.3.cloned.1.call-start = ((), (), s32[]{:S(2)}) async-start(), calls=%async_computation.5 | async-start | bytes 12582912 | tf_op jit(solution)/shard_map/psum | solution.py:9
  56.5 2.8 copy-start
  62.4 1.6 copy-start.2
  62.4 119.4 %all-gather.5.cloned.1.call-start = ((), (), s32[]{:S(2)}) async-start(), calls=%async_computation.1 | async-start | bytes 4718592 | tf_op jit(solution)/shard_map/all_gather | solution.py:20
  65.5 145.5 %all-gather.7.cloned.1.call-start = ((), (), s32[]{:S(2)}) async-start(), calls=%async_computation.2 | async-start | bytes 4718592 | tf_op jit(solution)/shard_map/all_gather | solution.py:20
  66.1 218.3 %all-gather.9.cloned.1.call-start = ((), (), s32[]{:S(2)}) async-start(), calls=%async_computation.3 | async-start | bytes 4718592 | tf_op jit(solution)/shard_map/all_gather | solution.py:20
  66.6 291.3 %all-gather.11.cloned.1.call-start = ((), (), s32[]{:S(2)}) async-start(), calls=%async_computation.4 | async-start | bytes 4718592 | tf_op jit(solution)/shard_map/all_gather | solution.py:20
  181.8 29.1 %copy-start.4 = (bf16[384,2048]{0,1:T(8,128)(2,1)S(1)}, bf16[384,2048]{0,1:T(8,128)(2,1)}, u32[]{:S(2)}) copy-start(bf16[384,2048]{0,1:T(8,128)(2,1)} %get-tuple-element.6) | copy-start | bytes 4718596
  284.4 73.5 %copy-start.1 = (bf16[384,2048]{0,1:T(8,128)(2,1)S(1)}, bf16[384,2048]{0,1:T(8,128)(2,1)}, u32[]{:S(2)}) copy-start(bf16[384,2048]{0,1:T(8,128)(2,1)} %get-tuple-element.8) | copy-start | bytes 4718596
  284.4 73.5 %copy-start.3 = (f32[384,1024]{1,0:T(8,128)S(1)}, f32[384,1024]{1,0:T(8,128)}, u32[]{:S(2)}) copy-start(f32[384,1024]{1,0:T(8,128)} %param.5) | copy-start | bytes 4718596
Sparse Core Ops, SparseCore 0:
  62.5 119.2 all-reduce.2
Sparse Core Ops, SparseCore 1:
  65.5 72.0 all-gather.4
  139.6 71.3 all-gather.6
  213.0 71.3 all-gather.8
  286.5 71.3 all-gather.10
where the time goes:
time: 372 us
  waiting for transfers between devices  313 us (84%)
  matrix products  23.2 us (6%)
  between operations  15.1 us (4%)
  local copies, waits for them, and re-layouts  11.4 us (3%)
  starting transfers between devices  7.49 us (2%)
    all_gather x4, waiting for transfers between devices, per_device(): panel_ints = lax.all_gather(stacked[column], 'wide', axis=0, tiled=True)  159 us
    psum x1, waiting for transfers between devices, broadcast(): return lax.psum(kept, axis)  114 us
    all_to_all x1, waiting for transfers between devices, per_device(): lax.all_to_all(amplitudes, 'wide', split_axis=0, concat_axis=1, tiled=True)  36.9 us
    dot_general x4, matrix products, per_device(): jnp.dot(panel, panel_ints, preferred_element_type=jnp.float32)  23.2 us
    select_n x4, local copies, waits for them, and re-layouts, broadcast(): jnp.where(lax.axis_index(axis) == source, value, 0).astype(value.dtype)  8.47 us
  transfers between devices with their start and end apart: 6, of which 5 were waited for; matrix products, arithmetic and copies ran while one was open for 5% of the time, Pallas kernels for 0%

commit v1 on v0

--- a/solution.py
+++ b/solution.py
@@ -1,7 +1,246 @@
+import functools
+
 import jax
 import jax.numpy as jnp
 from jax import lax
+from jax.experimental import pallas as pl
+from jax.experimental.pallas import tpu as pltpu
 from jax.sharding import PartitionSpec as P
+
+WIRE = jnp.float32
+CHUNKS = 4
+MESH = pl.DeviceIdType.MESH
+
+
+def kernel(nz, nc, a_ref, b_ref, r_ref, o_ref, a_all, b_all, part, send, up, dn,
+           al_s, bl_s, ay_s, ay_r, ax_s, ax_r, ac_s, ac_r, by_s, by_r, z_s, up_r, dn_r):
+    w, m = lax.axis_index("wide"), lax.axis_index("narrow")
+    z, y, x, c = w // 2, w % 2, m // 2, m % 2
+    rows, cols = r_ref.shape
+    ka, kb = a_ref.shape[1], b_ref.shape[0]
+    tile = cols // nc
+    to_y = (z * 2 + 1 - y, m)
+    to_x = (w, (1 - x) * 2 + c)
+    to_c = (w, x * 2 + 1 - c)
+    above, below = (w + 2, m), (w - 2, m)
+    high = (2 * z) // nz
+
+    def order(i):
+        return i + (1 - high) * (nz - 1 - 2 * i)
+
+    def piece(yy, xx, cc):
+        return pl.ds(pl.multiple_of((yy * 4 + xx * 2 + cc) * ka, ka), ka)
+
+    def rows_of(d, yy):
+        return a_ref.at[pl.ds(pl.multiple_of((d * 2 + yy) * rows, rows), rows), :]
+
+    def columns(n):
+        return pl.ds(pl.multiple_of(n * tile, tile), tile)
+
+    def remote(src, dst, s, r, to):
+        return pltpu.make_async_remote_copy(
+            src_ref=src, dst_ref=dst, send_sem=s, recv_sem=r, device_id=to, device_id_type=MESH)
+
+    def a_local(i):
+        d = order(i)
+        return pltpu.make_async_copy(rows_of(d, y), a_all.at[d, :, piece(y, x, c)], al_s.at[i])
+
+    def b_local(n):
+        return pltpu.make_async_copy(
+            b_ref.at[:, columns(n)], b_all.at[n, pl.ds(pl.multiple_of(y * kb, kb), kb)], bl_s.at[n])
+
+    def a_y(i):
+        d = order(i)
+        return remote(rows_of(d, 1 - y), a_all.at[d, :, piece(y, x, c)], ay_s.at[i], ay_r.at[i], to_y)
+
+    def a_x(i, j):
+        d = order(i)
+        src = rows_of(d, y) if j == 0 else a_all.at[d, :, piece(1 - y, x, c)]
+        dst = a_all.at[d, :, piece(y if j == 0 else 1 - y, x, c)]
+        return remote(src, dst, ax_s.at[i, j], ax_r.at[i, j], to_x)
+
+    def a_c(i, j):
+        d = order(i)
+        here = piece(y if j % 2 == 0 else 1 - y, x if j < 2 else 1 - x, c)
+        src = rows_of(d, y) if j == 0 else a_all.at[d, :, here]
+        return remote(src, a_all.at[d, :, here], ac_s.at[i, j], ac_r.at[i, j], to_c)
+
+    def b_y(n):
+        return remote(b_ref.at[:, columns(n)], b_all.at[n, pl.ds(pl.multiple_of(y * kb, kb), kb)],
+                      by_s.at[n], by_r.at[n], to_y)
+
+    def c_up(d, n):
+        return remote(send.at[d, n], up.at[d, n], z_s.at[d, n], up_r.at[d, n], above)
+
+    def c_dn(d, n):
+        return remote(send.at[d, n], dn.at[d, n], z_s.at[d, n], dn_r.at[d, n], below)
+
+    for i in range(nz):
+        a_local(i).start()
+    for n in range(nc):
+        b_local(n).start()
+
+    barrier = pltpu.get_barrier_semaphore()
+    for to in (to_y, to_x, to_c):
+        pl.semaphore_signal(barrier, inc=1, device_id=to, device_id_type=MESH)
+
+    @pl.when(z > 0)
+    def _():
+        pl.semaphore_signal(barrier, inc=1, device_id=below, device_id_type=MESH)
+
+    @pl.when(z < nz - 1)
+    def _():
+        pl.semaphore_signal(barrier, inc=1, device_id=above, device_id_type=MESH)
+
+    pl.semaphore_wait(barrier, 3 + (z + nz - 1) // nz + (2 * nz - 2 - z) // nz)
+
+    def first(i):
+        a_y(i).start()
+        a_x(i, 0).start()
+        a_c(i, 0).start()
+
+    first(0)
+    first(1)
+    b_y(0).start()
+
+    def step(t, carry):
+        n, i = t // nz, t % nz
+        d = order(i)
+
+        @pl.when(n == 0)
+        def _():
+            a_y(i).wait_recv()
+            a_x(i, 1).start()
+            a_c(i, 1).start()
+
+            @pl.when(i + 2 < nz)
+            def _():
+                first(i + 2)
+
+            a_x(i, 0).wait_recv()
+            a_c(i, 2).start()
+            a_x(i, 1).wait_recv()
+            a_c(i, 3).start()
+            a_local(i).wait()
+            for j in range(4):
+                a_c(i, j).wait_recv()
+
+        @pl.when(i == 0)
+        def _():
+            @pl.when(n + 1 < nc)
+            def _():
+                b_y(n + 1).start()
+
+            b_local(n).wait()
+            b_y(n).wait_recv()
+
+        part[...] = jnp.dot(a_all[d], b_all[n], preferred_element_type=jnp.float32)
+
+        @pl.when(d == z)
+        def _():
+            o_ref[:, columns(n)] = r_ref[:, columns(n)] + part[...]
+
+        @pl.when(d > z)
+        def _():
+            @pl.when(z > 0)
+            def _():
+                c_up(d, n).wait_recv()
+                send[d, n] = (part[...] + up[d, n].astype(jnp.float32)).astype(send.dtype)
+
+            @pl.when(z == 0)
+            def _():
+                send[d, n] = part[...].astype(send.dtype)
+
+            c_up(d, n).start()
+
+        @pl.when(d < z)
+        def _():
+            @pl.when(z < nz - 1)
+            def _():
+                c_dn(d, n).wait_recv()
+                send[d, n] = (part[...] + dn[d, n].astype(jnp.float32)).astype(send.dtype)
+
+            @pl.when(z == nz - 1)
+            def _():
+                send[d, n] = part[...].astype(send.dtype)
+
+            c_dn(d, n).start()
+
+        return carry
+
+    lax.fori_loop(0, nz * nc, step, 0)
+
+    def finish(n, carry):
+        @pl.when(z > 0)
+        def _():
+            c_up(z, n).wait_recv()
+            o_ref[:, columns(n)] += up[z, n].astype(jnp.float32)
+
+        @pl.when(z < nz - 1)
+        def _():
+            c_dn(z, n).wait_recv()
+            o_ref[:, columns(n)] += dn[z, n].astype(jnp.float32)
+
+        return carry
+
+    lax.fori_loop(0, nc, finish, 0)
+
+    def drain_a(i, carry):
+        a_y(i).wait_send()
+        for j in range(2):
+            a_x(i, j).wait_send()
+        for j in range(4):
+            a_c(i, j).wait_send()
+        return carry
+
+    def drain_b(n, carry):
+        b_y(n).wait_send()
+        return carry
+
+    def drain_c(t, carry):
+        d, n = t // nc, t % nc
+
+        @pl.when(d != z)
+        def _():
+            c_up(d, n).wait_send()
+
+        return carry
+
+    lax.fori_loop(0, nz, drain_a, 0)
+    lax.fori_loop(0, nc, drain_b, 0)
+    lax.fori_loop(0, nz * nc, drain_c, 0)
+
+
+def ladder_kernel(amplitudes, integrals, old_residual):
+    nz, nc = lax.axis_size("wide") // 2, CHUNKS
+    rows, cols = old_residual.shape
+    depth = 2 * integrals.shape[0]
+    tile = cols // nc
+    dma = pltpu.SemaphoreType.DMA
+    return pl.pallas_call(
+        functools.partial(kernel, nz, nc),
+        out_shape=jax.ShapeDtypeStruct((rows, cols), jnp.float32),
+        in_specs=[pl.BlockSpec(memory_space=pl.ANY)] * 2 + [pl.BlockSpec(memory_space=pltpu.VMEM)],
+        out_specs=pl.BlockSpec(memory_space=pltpu.VMEM),
+        scratch_shapes=[
+            pltpu.VMEM((nz, rows, depth), jnp.bfloat16),
+            pltpu.VMEM((nc, depth, tile), jnp.bfloat16),
+            pltpu.VMEM((rows, tile), jnp.float32),
+            pltpu.VMEM((nz, nc, rows, tile), WIRE),
+            pltpu.VMEM((nz, nc, rows, tile), WIRE),
+            pltpu.VMEM((nz, nc, rows, tile), WIRE),
+            dma((nz,)), dma((nc,)),
+            dma((nz,)), dma((nz,)),
+            dma((nz, 2)), dma((nz, 2)),
+            dma((nz, 4)), dma((nz, 4)),
+            dma((nc,)), dma((nc,)),
+            dma((nz, nc)), dma((nz, nc)), dma((nz, nc)),
+        ],
+        compiler_params=pltpu.CompilerParams(
+            collective_id=0, has_side_effects=True, vmem_limit_bytes=50 * 1024 * 1024),
+        cost_estimate=pl.CostEstimate(
+            flops=2 * nz * rows * depth * cols, bytes_accessed=8 * rows * cols, transcendentals=0),
+    )(amplitudes, integrals, old_residual)
 
 
 def broadcast(value, axis, source):
@@ -9,7 +248,7 @@
     return lax.psum(kept, axis)
 
 
-def per_device(amplitudes, integrals, old_residual):
+def ladder_gathered(amplitudes, integrals, old_residual):
     panels = lax.axis_size("narrow")
     sub_rows = integrals.shape[0] // panels
     stacked = integrals.reshape(panels, sub_rows, integrals.shape[1])
@@ -22,6 +261,12 @@
     return total
 
 
+def per_device(amplitudes, integrals, old_residual):
+    if amplitudes.shape[1] % 128 or lax.axis_size("narrow") != 4 or lax.axis_size("wide") > 8:
+        return ladder_gathered(amplitudes, integrals, old_residual)
+    return ladder_kernel(amplitudes, integrals, old_residual)
+
+
 def solution(mesh):
     placed = (P(None, ("wide", "narrow")), P("wide", "narrow"), P("wide", "narrow"))
     return jax.shard_map(

time: 372 us -> 140 us (0.38)
  waiting for transfers between devices: 313 us -> 0 us
  Pallas kernels: 0 us -> 137 us
  matrix products: 23.2 us -> 0 us
  between operations: 15.1 us -> 0.01 us
  local copies, waits for them, and re-layouts: 11.4 us -> 2.55 us
  starting transfers between devices: 7.49 us -> 0 us
    all_gather x4 -> x0, waiting for transfers between devices: 159 us -> none  [per_device(): panel_ints = lax.all_gather(stacked[column], 'wide', axis=0, tiled=True)]
    pallas_call x0 -> x1, Pallas kernels: none -> 137 us  [ladder_kernel(): pl.pallas_call(functools.partial(kernel, nz, nc), out_shape=jax.ShapeDtyp...]
    psum x1 -> x0, waiting for transfers between devices: 114 us -> none  [broadcast(): return lax.psum(kept, axis)]
    all_to_all x1 -> x0, waiting for transfers between devices: 36.9 us -> none  [per_device(): lax.all_to_all(amplitudes, 'wide', split_axis=0, concat_axis=1, tiled=True)]
    dot_general x4 -> x0, matrix products: 23.2 us -> none  [per_device(): jnp.dot(panel, panel_ints, preferred_element_type=jnp.float32)]
    select_n x4 -> x0, local copies, waits for them, and re-layouts: 8.47 us -> none  [broadcast(): jnp.where(lax.axis_index(axis) == source, value, 0).astype(value.dtype)]
    all_to_all x1 -> x0, starting transfers between devices: 7.28 us -> none  [per_device(): lax.all_to_all(amplitudes, 'wide', split_axis=0, concat_axis=1, tiled=True)]
  transfers between devices with their start and end apart: 6 -> 0, of which waited for: 5 -> 0; matrix products, arithmetic and copies ran while one was open for 5% -> 0% of each run, Pallas kernels for 0% -> 0%
where the time goes in v1:
time: 140 us
  Pallas kernels  137 us (98%)
  local copies, waits for them, and re-layouts  2.55 us (2%)
    pallas_call x1, Pallas kernels, ladder_kernel(): pl.pallas_call(functools.partial(kernel, nz, nc), out_shape=jax.ShapeDtyp...  137 us

profile of v1, /device:TPU:0, one launch (start us, length us, event | category | flops | bytes accessed | tf_op | source)
XLA Modules:
  0.0 140.0 jit_solution(11821461901017462434)
XLA Ops:
  0.0 0.0 copy-start
  0.0 1.4 %copy-done = bf16[3072,256]{1,0:T(8,128)(2,1)S(1)} copy-done((bf16[3072,256]{1,0:T(8,128)(2,1)S(1)}, bf16[3072,256]{1,0:T(8,128)(2,1)}, u32[]{:S(2)}) %copy-start) | copy-done | bytes 1572888
  1.4 137.4 %shard_map.37 = f32[384,1024]{1,0:T(8,128)S(1)} custom-call(bf16[3072,256]{1,0:T(8,128)(2,1)S(1)} %copy-done, bf16[1024,1024]{1,0:T(8,128)(2,1)} %b_ref.1, f32[384,1024]{1,0:T(8,128)} %r_ref.1), custom_call_target="tpu_custom_call" | custom-call | flops 6442450944 | bytes 3145728 | tf_op jit(solution)/shard_map/pallas_call | solution.py:220
  138.8 1.1 copy.5
Async XLA Ops:
  0.0 1.4 %copy-start = (bf16[3072,256]{1,0:T(8,128)(2,1)S(1)}, bf16[3072,256]{1,0:T(8,128)(2,1)}, u32[]{:S(2)}) copy-start(bf16[3072,256]{1,0:T(8,128)(2,1)} %a_ref.1) | copy-start | bytes 4718596

commit v2 on v1

--- a/solution.py
+++ b/solution.py
@@ -7,9 +7,30 @@
 from jax.experimental.pallas import tpu as pltpu
 from jax.sharding import PartitionSpec as P
 
-WIRE = jnp.float32
+SCALE_ROWS = 16
+KEEP = 46000.0
 CHUNKS = 4
 MESH = pl.DeviceIdType.MESH
+
+
+def encode(ref, d, n, value):
+    rows = value.shape[0]
+    peak = jnp.max(jnp.abs(value), axis=0, keepdims=True)
+    scale = (peak * 1.01 + 1e-30).astype(jnp.bfloat16)
+    q = value * (KEEP / scale.astype(jnp.float32))
+    q2 = q * q
+    q4 = q2 * q2
+    ref[d, n, :rows] = (q4 * q2 * (q * jnp.abs(q))).astype(jnp.bfloat16)
+    ref[d, n, rows:] = jnp.broadcast_to(scale, (SCALE_ROWS, value.shape[1]))
+
+
+def decode(ref, d, n, rows):
+    code = ref[d, n, :rows].astype(jnp.float32)
+    scale = ref[d, n, rows:].astype(jnp.float32)[:1]
+    r1 = lax.rsqrt(jnp.maximum(jnp.abs(code), 1.2e-38))
+    r2 = lax.rsqrt(r1)
+    root = r2 * lax.rsqrt(r2)
+    return jnp.where(code < 0, -root, root) * (scale * (1.0 / KEEP))
 
 
 def kernel(nz, nc, a_ref, b_ref, r_ref, o_ref, a_all, b_all, part, send, up, dn,
@@ -145,11 +166,11 @@
             @pl.when(z > 0)
             def _():
                 c_up(d, n).wait_recv()
-                send[d, n] = (part[...] + up[d, n].astype(jnp.float32)).astype(send.dtype)
+                encode(send, d, n, part[...] + decode(up, d, n, rows))
 
             @pl.when(z == 0)
             def _():
-                send[d, n] = part[...].astype(send.dtype)
+                encode(send, d, n, part[...])
 
             c_up(d, n).start()
 
@@ -158,11 +179,11 @@
             @pl.when(z < nz - 1)
             def _():
                 c_dn(d, n).wait_recv()
-                send[d, n] = (part[...] + dn[d, n].astype(jnp.float32)).astype(send.dtype)
+                encode(send, d, n, part[...] + decode(dn, d, n, rows))
 
             @pl.when(z == nz - 1)
             def _():
-                send[d, n] = part[...].astype(send.dtype)
+                encode(send, d, n, part[...])
 
             c_dn(d, n).start()
 
@@ -174,12 +195,12 @@
         @pl.when(z > 0)
         def _():
             c_up(z, n).wait_recv()
-            o_ref[:, columns(n)] += up[z, n].astype(jnp.float32)
+            o_ref[:, columns(n)] += decode(up, z, n, rows)
 
         @pl.when(z < nz - 1)
         def _():
             c_dn(z, n).wait_recv()
-            o_ref[:, columns(n)] += dn[z, n].astype(jnp.float32)
+            o_ref[:, columns(n)] += decode(dn, z, n, rows)
 
         return carry
 
@@ -226,9 +247,9 @@
             pltpu.VMEM((nz, rows, depth), jnp.bfloat16),
             pltpu.VMEM((nc, depth, tile), jnp.bfloat16),
             pltpu.VMEM((rows, tile), jnp.float32),
-            pltpu.VMEM((nz, nc, rows, tile), WIRE),
-            pltpu.VMEM((nz, nc, rows, tile), WIRE),
-            pltpu.VMEM((nz, nc, rows, tile), WIRE),
+            pltpu.VMEM((nz, nc, rows + SCALE_ROWS, tile), jnp.bfloat16),
+            pltpu.VMEM((nz, nc, rows + SCALE_ROWS, tile), jnp.bfloat16),
+            pltpu.VMEM((nz, nc, rows + SCALE_ROWS, tile), jnp.bfloat16),
             dma((nz,)), dma((nc,)),
             dma((nz,)), dma((nz,)),
             dma((nz, 2)), dma((nz, 2)),

time: 140 us -> 105 us (0.75)
  Pallas kernels: 137 us -> 103 us
    pallas_call x1, Pallas kernels: 137 us -> 103 us  [ladder_kernel(): pl.pallas_call(functools.partial(kernel, nz, nc), out_shape=jax.ShapeDtyp...]
where the time goes in v2:
time: 105 us
  Pallas kernels  103 us (98%)
  local copies, waits for them, and re-layouts  2.55 us (2%)
    pallas_call x1, Pallas kernels, ladder_kernel(): pl.pallas_call(functools.partial(kernel, nz, nc), out_shape=jax.ShapeDtyp...  103 us
    unnamed x3, local copies, waits for them, and re-layouts  2.55 us

profile of v2, /device:TPU:0, one launch (start us, length us, event | category | flops | bytes accessed | tf_op | source)
XLA Modules:
  0.0 105.2 jit_solution(1397334995326135801)
XLA Ops:
  0.0 0.0 copy-start
  0.0 1.4 %copy-done = bf16[3072,256]{1,0:T(8,128)(2,1)S(1)} copy-done((bf16[3072,256]{1,0:T(8,128)(2,1)S(1)}, bf16[3072,256]{1,0:T(8,128)(2,1)}, u32[]{:S(2)}) %copy-start) | copy-done | bytes 1572888
  1.4 102.7 %shard_map.37 = f32[384,1024]{1,0:T(8,128)S(1)} custom-call(bf16[3072,256]{1,0:T(8,128)(2,1)S(1)} %copy-done, bf16[1024,1024]{1,0:T(8,128)(2,1)} %b_ref.1, f32[384,1024]{1,0:T(8,128)} %r_ref.1), custom_call_target="tpu_custom_call" | custom-call | flops 6442450944 | bytes 3145728 | tf_op jit(solution)/shard_map/pallas_call | solution.py:241
  104.1 1.1 %copy.5 = f32[384,1024]{1,0:T(8,128)} copy(f32[384,1024]{1,0:T(8,128)S(1)} %shard_map.37) | data formatting | bytes 3145728
Async XLA Ops:
  0.0 1.4 %copy-start = (bf16[3072,256]{1,0:T(8,128)(2,1)S(1)}, bf16[3072,256]{1,0:T(8,128)(2,1)}, u32[]{:S(2)}) copy-start(bf16[3072,256]{1,0:T(8,128)(2,1)} %a_ref.1) | copy-start | bytes 4718596

commit v3 on v2

--- a/solution.py
+++ b/solution.py
@@ -9,7 +9,7 @@
 
 SCALE_ROWS = 16
 KEEP = 46000.0
-CHUNKS = 4
+CHUNKS = 8
 MESH = pl.DeviceIdType.MESH
 
 
@@ -34,7 +34,7 @@
 
 
 def kernel(nz, nc, a_ref, b_ref, r_ref, o_ref, a_all, b_all, part, send, up, dn,
-           al_s, bl_s, ay_s, ay_r, ax_s, ax_r, ac_s, ac_r, by_s, by_r, z_s, up_r, dn_r):
+           r_s, al_s, bl_s, ay_s, ay_r, ax_s, ax_r, ac_s, ac_r, by_s, by_r, z_s, up_r, dn_r):
     w, m = lax.axis_index("wide"), lax.axis_index("narrow")
     z, y, x, c = w // 2, w % 2, m // 2, m % 2
     rows, cols = r_ref.shape
@@ -96,10 +96,12 @@
     def c_dn(d, n):
         return remote(send.at[d, n], dn.at[d, n], z_s.at[d, n], dn_r.at[d, n], below)
 
+    residual = pltpu.make_async_copy(r_ref, o_ref, r_s)
     for i in range(nz):
         a_local(i).start()
     for n in range(nc):
         b_local(n).start()
+    residual.start()
 
     barrier = pltpu.get_barrier_semaphore()
     for to in (to_y, to_x, to_c):
@@ -123,6 +125,7 @@
     first(0)
     first(1)
     b_y(0).start()
+    residual.wait()
 
     def step(t, carry):
         n, i = t // nz, t % nz
@@ -159,7 +162,7 @@
 
         @pl.when(d == z)
         def _():
-            o_ref[:, columns(n)] = r_ref[:, columns(n)] + part[...]
+            o_ref[:, columns(n)] += part[...]
 
         @pl.when(d > z)
         def _():
@@ -241,7 +244,7 @@
     return pl.pallas_call(
         functools.partial(kernel, nz, nc),
         out_shape=jax.ShapeDtypeStruct((rows, cols), jnp.float32),
-        in_specs=[pl.BlockSpec(memory_space=pl.ANY)] * 2 + [pl.BlockSpec(memory_space=pltpu.VMEM)],
+        in_specs=[pl.BlockSpec(memory_space=pl.ANY)] * 3,
         out_specs=pl.BlockSpec(memory_space=pltpu.VMEM),
         scratch_shapes=[
             pltpu.VMEM((nz, rows, depth), jnp.bfloat16),
@@ -250,7 +253,7 @@
             pltpu.VMEM((nz, nc, rows + SCALE_ROWS, tile), jnp.bfloat16),
             pltpu.VMEM((nz, nc, rows + SCALE_ROWS, tile), jnp.bfloat16),
             pltpu.VMEM((nz, nc, rows + SCALE_ROWS, tile), jnp.bfloat16),
-            dma((nz,)), dma((nc,)),
+            dma, dma((nz,)), dma((nc,)),
             dma((nz,)), dma((nz,)),
             dma((nz, 2)), dma((nz, 2)),
             dma((nz, 4)), dma((nz, 4)),

time: 105 us -> 105 us (level)
  no operation moved by 1% of the time
where the time goes in v3:
time: 105 us
  Pallas kernels  102 us (97%)
  local copies, waits for them, and re-layouts  2.55 us (2%)
    pallas_call x1, Pallas kernels, ladder_kernel(): pl.pallas_call(functools.partial(kernel, nz, nc), out_shape=jax.ShapeDtyp...  102 us
    unnamed x3, local copies, waits for them, and re-layouts  2.55 us

profile of v3, /device:TPU:0, one launch (start us, length us, event | category | flops | bytes accessed | tf_op | source)
XLA Modules:
  0.0 104.8 jit_solution(7263451231883776468)
XLA Ops:
  0.0 0.0 copy-start
  0.0 1.4 %copy-done = bf16[3072,256]{1,0:T(8,128)(2,1)S(1)} copy-done((bf16[3072,256]{1,0:T(8,128)(2,1)S(1)}, bf16[3072,256]{1,0:T(8,128)(2,1)}, u32[]{:S(2)}) %copy-start) | copy-done | bytes 1572888
  1.4 102.3 %shard_map.37 = f32[384,1024]{1,0:T(8,128)S(1)} custom-call(bf16[3072,256]{1,0:T(8,128)(2,1)S(1)} %copy-done, bf16[1024,1024]{1,0:T(8,128)(2,1)} %b_ref.1, f32[384,1024]{1,0:T(8,128)} %r_ref.1), custom_call_target="tpu_custom_call" | custom-call | flops 6442450944 | bytes 3145728 | tf_op jit(solution)/shard_map/pallas_call | solution.py:244
  103.7 1.1 %copy.5 = f32[384,1024]{1,0:T(8,128)} copy(f32[384,1024]{1,0:T(8,128)S(1)} %shard_map.37) | data formatting | bytes 3145728
Async XLA Ops:
  0.0 1.4 %copy-start = (bf16[3072,256]{1,0:T(8,128)(2,1)S(1)}, bf16[3072,256]{1,0:T(8,128)(2,1)}, u32[]{:S(2)}) copy-start(bf16[3072,256]{1,0:T(8,128)(2,1)} %a_ref.1) | copy-start | bytes 4718596

commit v4 on v3

--- a/solution.py
+++ b/solution.py
@@ -10,6 +10,7 @@
 SCALE_ROWS = 16
 KEEP = 46000.0
 CHUNKS = 8
+AHEAD = 3
 MESH = pl.DeviceIdType.MESH
 
 
@@ -46,8 +47,12 @@
     above, below = (w + 2, m), (w - 2, m)
     high = (2 * z) // nz
 
+    own = z + (1 - high) * (nz - 1 - 2 * z)
+
     def order(i):
-        return i + (1 - high) * (nz - 1 - 2 * i)
+        last = (i + 1) // nz
+        k = last * own + (1 - last) * (i + (i + nz - own) // nz)
+        return k + (1 - high) * (nz - 1 - 2 * k)
 
     def piece(yy, xx, cc):
         return pl.ds(pl.multiple_of((yy * 4 + xx * 2 + cc) * ka, ka), ka)
@@ -117,52 +122,84 @@
 
     pl.semaphore_wait(barrier, 3 + (z + nz - 1) // nz + (2 * nz - 2 - z) // nz)
 
-    def first(i):
-        a_y(i).start()
-        a_x(i, 0).start()
-        a_c(i, 0).start()
-
-    first(0)
-    first(1)
-    b_y(0).start()
+    queue = []
+    for e in range(nz - 1):
+        queue += [("a", e), ("b", e)]
+    queue += [("b", n) for n in range(nz - 1, nc - 1)] + [("a", nz - 1), ("b", nc - 1)]
+
+    def start_y(k):
+        if k < len(queue):
+            (a_y if queue[k][0] == "a" else b_y)(queue[k][1]).start()
+
+    def start_own(i):
+        if i < nz:
+            a_x(i, 0).start()
+            a_c(i, 0).start()
+
+    def a_arrives(i):
+        a_y(i).wait_recv()
+        start_y(queue.index(("a", i)) + AHEAD)
+        a_x(i, 1).start()
+        a_c(i, 1).start()
+        start_own(i + 2)
+
+    def b_arrives(n):
+        b_local(n).wait()
+        b_y(n).wait_recv()
+        start_y(queue.index(("b", n)) + AHEAD)
+
+    def a_complete(i):
+        a_x(i, 0).wait_recv()
+        a_c(i, 2).start()
+        a_x(i, 1).wait_recv()
+        a_c(i, 3).start()
+        a_local(i).wait()
+        for j in range(4):
+            a_c(i, j).wait_recv()
+
+    for k in range(AHEAD):
+        start_y(k)
+    start_own(0)
+    start_own(1)
     residual.wait()
 
+    head = [(0, 0)]
+    for e in range(1, nz - 1):
+        head += [(i, e) for i in range(e)] + [(e, n) for n in range(e + 1)]
+    sends = (nz - 1) * nc
+
     def step(t, carry):
-        n, i = t // nz, t % nz
-        d = order(i)
-
-        @pl.when(n == 0)
-        def _():
-            a_y(i).wait_recv()
-            a_x(i, 1).start()
-            a_c(i, 1).start()
-
-            @pl.when(i + 2 < nz)
-            def _():
-                first(i + 2)
-
-            a_x(i, 0).wait_recv()
-            a_c(i, 2).start()
-            a_x(i, 1).wait_recv()
-            a_c(i, 3).start()
-            a_local(i).wait()
-            for j in range(4):
-                a_c(i, j).wait_recv()
-
-        @pl.when(i == 0)
-        def _():
-            @pl.when(n + 1 < nc)
-            def _():
-                b_y(n + 1).start()
-
-            b_local(n).wait()
-            b_y(n).wait_recv()
+        i = (t - len(head)) % (nz - 1)
+        n = nz - 1 + (t - len(head)) // (nz - 1)
+        for k, (head_i, head_n) in enumerate(head):
+            i = jnp.where(t == k, head_i, i)
+            n = jnp.where(t == k, head_n, n)
+        d = order(i)
+
+        @pl.when(t == 0)
+        def _():
+            a_arrives(0)
+            b_arrives(0)
+            a_complete(0)
+
+        for e in range(1, nz - 1):
+            @pl.when(t == head.index((0, e)))
+            def _():
+                a_arrives(e)
+                b_arrives(e)
+
+            @pl.when(t == head.index((e, 0)))
+            def _():
+                a_complete(e)
+
+        for e in range(nz - 1, nc):
+            @pl.when(t == len(head) + (e - nz + 1) * (nz - 1))
+            def _():
+                if e == nc - 1:
+                    a_arrives(nz - 1)
+                b_arrives(e)
 
         part[...] = jnp.dot(a_all[d], b_all[n], preferred_element_type=jnp.float32)
-
-        @pl.when(d == z)
-        def _():
-            o_ref[:, columns(n)] += part[...]
 
         @pl.when(d > z)
         def _():
@@ -192,9 +229,13 @@
 
         return carry
 
-    lax.fori_loop(0, nz * nc, step, 0)
+    lax.fori_loop(0, sends, step, 0)
+
+    a_complete(nz - 1)
 
     def finish(n, carry):
+        o_ref[:, columns(n)] += jnp.dot(a_all[z], b_all[n], preferred_element_type=jnp.float32)
+
         @pl.when(z > 0)
         def _():
             c_up(z, n).wait_recv()

time: 105 us -> 93 us (0.89); the launches traced: 105 us -> 91.3 us
  Pallas kernels: 102 us -> 88.7 us
    pallas_call x1, Pallas kernels: 102 us -> 88.7 us  [ladder_kernel(): pl.pallas_call(functools.partial(kernel, nz, nc), out_shape=jax.ShapeDtyp...]
where the time goes in v4:
time: 93 us; the launch traced here: 91.3 us
  Pallas kernels  88.7 us (95%)
  local copies, waits for them, and re-layouts  2.55 us (3%)
    pallas_call x1, Pallas kernels, ladder_kernel(): pl.pallas_call(functools.partial(kernel, nz, nc), out_shape=jax.ShapeDtyp...  88.7 us
    unnamed x3, local copies, waits for them, and re-layouts  2.55 us

profile of v4, /device:TPU:0, one launch (start us, length us, event | category | flops | bytes accessed | tf_op | source)
XLA Modules:
  0.0 91.3 jit_solution(649961169444847779)
XLA Ops:
  0.0 0.0 copy-start
  0.0 1.4 %copy-done = bf16[3072,256]{1,0:T(8,128)(2,1)S(1)} copy-done((bf16[3072,256]{1,0:T(8,128)(2,1)S(1)}, bf16[3072,256]{1,0:T(8,128)(2,1)}, u32[]{:S(2)}) %copy-start) | copy-done | bytes 1572888
  1.4 88.7 %shard_map.37 = f32[384,1024]{1,0:T(8,128)S(1)} custom-call(bf16[3072,256]{1,0:T(8,128)(2,1)S(1)} %copy-done, bf16[1024,1024]{1,0:T(8,128)(2,1)} %b_ref.1, f32[384,1024]{1,0:T(8,128)} %r_ref.1), custom_call_target="tpu_custom_call" | custom-call | flops 6442450944 | bytes 3145728 | tf_op jit(solution)/shard_map/pallas_call | solution.py:285
  90.1 1.1 %copy.5 = f32[384,1024]{1,0:T(8,128)} copy(f32[384,1024]{1,0:T(8,128)S(1)} %shard_map.37) | data formatting | bytes 3145728
Async XLA Ops:
  0.0 1.4 %copy-start = (bf16[3072,256]{1,0:T(8,128)(2,1)S(1)}, bf16[3072,256]{1,0:T(8,128)(2,1)}, u32[]{:S(2)}) copy-start(bf16[3072,256]{1,0:T(8,128)(2,1)} %a_ref.1) | copy-start | bytes 4718596

commit v5 on v4

--- a/solution.py
+++ b/solution.py
@@ -10,7 +10,7 @@
 SCALE_ROWS = 16
 KEEP = 46000.0
 CHUNKS = 8
-AHEAD = 3
+AHEAD = 6
 MESH = pl.DeviceIdType.MESH
 
 
@@ -125,7 +125,7 @@
     queue = []
     for e in range(nz - 1):
         queue += [("a", e), ("b", e)]
-    queue += [("b", n) for n in range(nz - 1, nc - 1)] + [("a", nz - 1), ("b", nc - 1)]
+    queue += [("b", n) for n in range(nz - 1, nc)] + [("a", nz - 1)]
 
     def start_y(k):
         if k < len(queue):
@@ -195,8 +195,6 @@
         for e in range(nz - 1, nc):
             @pl.when(t == len(head) + (e - nz + 1) * (nz - 1))
             def _():
-                if e == nc - 1:
-                    a_arrives(nz - 1)
                 b_arrives(e)
 
         part[...] = jnp.dot(a_all[d], b_all[n], preferred_element_type=jnp.float32)
@@ -231,6 +229,7 @@
 
     lax.fori_loop(0, sends, step, 0)
 
+    a_arrives(nz - 1)
     a_complete(nz - 1)
 
     def finish(n, carry):
@@ -302,7 +301,7 @@
             dma((nz, nc)), dma((nz, nc)), dma((nz, nc)),
         ],
         compiler_params=pltpu.CompilerParams(
-            collective_id=0, has_side_effects=True, vmem_limit_bytes=50 * 1024 * 1024),
+            collective_id=0, has_side_effects=True, vmem_limit_bytes=62 * 1024 * 1024),
         cost_estimate=pl.CostEstimate(
             flops=2 * nz * rows * depth * cols, bytes_accessed=8 * rows * cols, transcendentals=0),
     )(amplitudes, integrals, old_residual)

time: 93 us -> 101 us (1.086)
  the two profiles are of different devices: /device:TPU:0 before, /device:TPU:9 now
where the time goes in v5:
time: 101 us
  Pallas kernels  98 us (97%)
  local copies, waits for them, and re-layouts  2.73 us (3%)
    pallas_call x1, Pallas kernels, ladder_kernel(): pl.pallas_call(functools.partial(kernel, nz, nc), out_shape=jax.ShapeDtyp...  98 us
    unnamed x1, local copies, waits for them, and re-layouts  2.73 us

profile of v5, /device:TPU:9, one launch (start us, length us, event | category | flops | bytes accessed | tf_op | source)
XLA Modules:
  0.0 100.8 jit_solution(9016851628553468446)
XLA Ops:
  0.0 98.0 %shard_map.37 = f32[384,1024]{1,0:T(8,128)} custom-call(bf16[3072,256]{1,0:T(8,128)(2,1)} %a_ref.1, bf16[1024,1024]{1,0:T(8,128)(2,1)} %b_ref.1, f32[384,1024]{1,0:T(8,128)} %r_ref.1), custom_call_target="tpu_custom_call" | custom-call | flops 6442450944 | bytes 3145728 | tf_op jit(solution)/shard_map/pallas_call | solution.py:284
  98.1 2.7 %copy.5 = f32[384,1024]{1,0:T(8,128)} copy(f32[384,1024]{1,0:T(8,128)} %shard_map.37) | data formatting | bytes 3145728

commit v6 on v5

--- a/solution.py
+++ b/solution.py
@@ -10,7 +10,7 @@
 SCALE_ROWS = 16
 KEEP = 46000.0
 CHUNKS = 8
-AHEAD = 6
+AHEAD = 2
 MESH = pl.DeviceIdType.MESH
 
 
@@ -55,7 +55,7 @@
         return k + (1 - high) * (nz - 1 - 2 * k)
 
     def piece(yy, xx, cc):
-        return pl.ds(pl.multiple_of((yy * 4 + xx * 2 + cc) * ka, ka), ka)
+        return yy * 4 + xx * 2 + cc
 
     def rows_of(d, yy):
         return a_ref.at[pl.ds(pl.multiple_of((d * 2 + yy) * rows, rows), rows), :]
@@ -69,7 +69,7 @@
 
     def a_local(i):
         d = order(i)
-        return pltpu.make_async_copy(rows_of(d, y), a_all.at[d, :, piece(y, x, c)], al_s.at[i])
+        return pltpu.make_async_copy(rows_of(d, y), a_all.at[d, piece(y, x, c)], al_s.at[i])
 
     def b_local(n):
         return pltpu.make_async_copy(
@@ -77,23 +77,23 @@
 
     def a_y(i):
         d = order(i)
-        return remote(rows_of(d, 1 - y), a_all.at[d, :, piece(y, x, c)], ay_s.at[i], ay_r.at[i], to_y)
+        return remote(rows_of(d, 1 - y), a_all.at[d, piece(y, x, c)], ay_s.at[i], ay_r.at[i], to_y)
 
     def a_x(i, j):
         d = order(i)
-        src = rows_of(d, y) if j == 0 else a_all.at[d, :, piece(1 - y, x, c)]
-        dst = a_all.at[d, :, piece(y if j == 0 else 1 - y, x, c)]
+        src = rows_of(d, y) if j == 0 else a_all.at[d, piece(1 - y, x, c)]
+        dst = a_all.at[d, piece(y if j == 0 else 1 - y, x, c)]
         return remote(src, dst, ax_s.at[i, j], ax_r.at[i, j], to_x)
 
     def a_c(i, j):
         d = order(i)
         here = piece(y if j % 2 == 0 else 1 - y, x if j < 2 else 1 - x, c)
-        src = rows_of(d, y) if j == 0 else a_all.at[d, :, here]
-        return remote(src, a_all.at[d, :, here], ac_s.at[i, j], ac_r.at[i, j], to_c)
+        src = rows_of(d, y) if j == 0 else a_all.at[d, here]
+        return remote(src, a_all.at[d, here], ac_s.at[i, j], ac_r.at[i, j], to_c)
 
     def b_y(n):
-        return remote(b_ref.at[:, columns(n)], b_all.at[n, pl.ds(pl.multiple_of(y * kb, kb), kb)],
-                      by_s.at[n], by_r.at[n], to_y)
+        half = b_all.at[n, pl.ds(pl.multiple_of(y * kb, kb), kb)]
+        return remote(half, half, by_s.at[n], by_r.at[n], to_y)
 
     def c_up(d, n):
         return remote(send.at[d, n], up.at[d, n], z_s.at[d, n], up_r.at[d, n], above)
@@ -102,10 +102,14 @@
         return remote(send.at[d, n], dn.at[d, n], z_s.at[d, n], dn_r.at[d, n], below)
 
     residual = pltpu.make_async_copy(r_ref, o_ref, r_s)
+    def product(d, n):
+        left = jnp.concatenate([a_all[d, p] for p in range(8)], axis=1)
+        return jnp.dot(left, b_all[n], preferred_element_type=jnp.float32)
+
+    for n in range(nc):
+        b_local(n).start()
     for i in range(nz):
         a_local(i).start()
-    for n in range(nc):
-        b_local(n).start()
     residual.start()
 
     barrier = pltpu.get_barrier_semaphore()
@@ -129,7 +133,10 @@
 
     def start_y(k):
         if k < len(queue):
-            (a_y if queue[k][0] == "a" else b_y)(queue[k][1]).start()
+            kind, e = queue[k]
+            if kind == "b":
+                b_local(e).wait()
+            (a_y if kind == "a" else b_y)(e).start()
 
     def start_own(i):
         if i < nz:
@@ -144,7 +151,6 @@
         start_own(i + 2)
 
     def b_arrives(n):
-        b_local(n).wait()
         b_y(n).wait_recv()
         start_y(queue.index(("b", n)) + AHEAD)
 
@@ -197,7 +203,7 @@
             def _():
                 b_arrives(e)
 
-        part[...] = jnp.dot(a_all[d], b_all[n], preferred_element_type=jnp.float32)
+        part[...] = product(d, n)
 
         @pl.when(d > z)
         def _():
@@ -233,7 +239,7 @@
     a_complete(nz - 1)
 
     def finish(n, carry):
-        o_ref[:, columns(n)] += jnp.dot(a_all[z], b_all[n], preferred_element_type=jnp.float32)
+        o_ref[:, columns(n)] += product(z, n)
 
         @pl.when(z > 0)
         def _():
@@ -287,7 +293,7 @@
         in_specs=[pl.BlockSpec(memory_space=pl.ANY)] * 3,
         out_specs=pl.BlockSpec(memory_space=pltpu.VMEM),
         scratch_shapes=[
-            pltpu.VMEM((nz, rows, depth), jnp.bfloat16),
+            pltpu.VMEM((nz, 8, rows, amplitudes.shape[1]), jnp.bfloat16),
             pltpu.VMEM((nc, depth, tile), jnp.bfloat16),
             pltpu.VMEM((rows, tile), jnp.float32),
             pltpu.VMEM((nz, nc, rows + SCALE_ROWS, tile), jnp.bfloat16),

time: 101 us -> 101 us (level)
  no operation moved by 1% of the time
where the time goes in v6:
time: 101 us
  Pallas kernels  98 us (97%)
  local copies, waits for them, and re-layouts  2.73 us (3%)
    pallas_call x1, Pallas kernels, ladder_kernel(): pl.pallas_call(functools.partial(kernel, nz, nc), out_shape=jax.ShapeDtyp...  98 us
    unnamed x1, local copies, waits for them, and re-layouts  2.73 us

profile of v6, /device:TPU:9, one launch (start us, length us, event | category | flops | bytes accessed | tf_op | source)
XLA Modules:
  0.0 100.7 jit_solution(7262942927968984572)
XLA Ops:
  0.0 98.0 %shard_map.37 = f32[384,1024]{1,0:T(8,128)} custom-call(bf16[3072,256]{1,0:T(8,128)(2,1)} %a_ref.1, bf16[1024,1024]{1,0:T(8,128)(2,1)} %b_ref.1, f32[384,1024]{1,0:T(8,128)} %r_ref.1), custom_call_target="tpu_custom_call" | custom-call | flops 6442450944 | bytes 3145728 | tf_op jit(solution)/shard_map/pallas_call | solution.py:290
  98.0 2.7 %copy.5 = f32[384,1024]{1,0:T(8,128)} copy(f32[384,1024]{1,0:T(8,128)} %shard_map.37) | data formatting | bytes 3145728

commit v7 on v6

--- a/solution.py
+++ b/solution.py
@@ -10,7 +10,7 @@
 SCALE_ROWS = 16
 KEEP = 46000.0
 CHUNKS = 8
-AHEAD = 2
+AHEAD = 3
 MESH = pl.DeviceIdType.MESH
 
 
@@ -129,7 +129,7 @@
     queue = []
     for e in range(nz - 1):
         queue += [("a", e), ("b", e)]
-    queue += [("b", n) for n in range(nz - 1, nc)] + [("a", nz - 1)]
+    queue += [("b", n) for n in range(nz - 1, nc - 2)] + [("a", nz - 1), ("b", nc - 2), ("b", nc - 1)]
 
     def start_y(k):
         if k < len(queue):
@@ -174,6 +174,23 @@
         head += [(i, e) for i in range(e)] + [(e, n) for n in range(e + 1)]
     sends = (nz - 1) * nc
 
+    def own_product(n, carry):
+        o_ref[:, columns(n)] += product(z, n)
+        return carry
+
+    def add_arrivals(n, carry):
+        @pl.when(z > 0)
+        def _():
+            c_up(z, n).wait_recv()
+            o_ref[:, columns(n)] += decode(up, z, n, rows)
+
+        @pl.when(z < nz - 1)
+        def _():
+            c_dn(z, n).wait_recv()
+            o_ref[:, columns(n)] += decode(dn, z, n, rows)
+
+        return carry
+
     def step(t, carry):
         i = (t - len(head)) % (nz - 1)
         n = nz - 1 + (t - len(head)) // (nz - 1)
@@ -201,6 +218,12 @@
         for e in range(nz - 1, nc):
             @pl.when(t == len(head) + (e - nz + 1) * (nz - 1))
             def _():
+                if e == nc - 2:
+                    a_arrives(nz - 1)
+                if e == nc - 1:
+                    a_complete(nz - 1)
+                    lax.fori_loop(0, nc - 1, own_product, 0)
+                    lax.fori_loop(0, nc - 4, add_arrivals, 0)
                 b_arrives(e)
 
         part[...] = product(d, n)
@@ -235,25 +258,8 @@
 
     lax.fori_loop(0, sends, step, 0)
 
-    a_arrives(nz - 1)
-    a_complete(nz - 1)
-
-    def finish(n, carry):
-        o_ref[:, columns(n)] += product(z, n)
-
-        @pl.when(z > 0)
-        def _():
-            c_up(z, n).wait_recv()
-            o_ref[:, columns(n)] += decode(up, z, n, rows)
-
-        @pl.when(z < nz - 1)
-        def _():
-            c_dn(z, n).wait_recv()
-            o_ref[:, columns(n)] += decode(dn, z, n, rows)
-
-        return carry
-
-    lax.fori_loop(0, nc, finish, 0)
+    own_product(nc - 1, 0)
+    lax.fori_loop(nc - 4, nc, add_arrivals, 0)
 
     def drain_a(i, carry):
         a_y(i).wait_send()
@@ -307,7 +313,7 @@
             dma((nz, nc)), dma((nz, nc)), dma((nz, nc)),
         ],
         compiler_params=pltpu.CompilerParams(
-            collective_id=0, has_side_effects=True, vmem_limit_bytes=62 * 1024 * 1024),
+            collective_id=0, has_side_effects=True, vmem_limit_bytes=50 * 1024 * 1024),
         cost_estimate=pl.CostEstimate(
             flops=2 * nz * rows * depth * cols, bytes_accessed=8 * rows * cols, transcendentals=0),
     )(amplitudes, integrals, old_residual)

time: 101 us -> 96.9 us (0.959)
  the two profiles are of different devices: /device:TPU:9 before, /device:TPU:0 now
where the time goes in v7:
time: 96.9 us; the launch traced here: 96.7 us
  Pallas kernels  94.2 us (97%)
  local copies, waits for them, and re-layouts  2.55 us (3%)
    pallas_call x1, Pallas kernels, ladder_kernel(): pl.pallas_call(functools.partial(kernel, nz, nc), out_shape=jax.ShapeDtyp...  94.2 us
    unnamed x3, local copies, waits for them, and re-layouts  2.55 us

profile of v7, /device:TPU:0, one launch (start us, length us, event | category | flops | bytes accessed | tf_op | source)
XLA Modules:
  0.0 96.7 jit_solution(9877765029504819656)
XLA Ops:
  0.0 0.0 copy-start
  0.0 1.4 %copy-done = bf16[3072,256]{1,0:T(8,128)(2,1)S(1)} copy-done((bf16[3072,256]{1,0:T(8,128)(2,1)S(1)}, bf16[3072,256]{1,0:T(8,128)(2,1)}, u32[]{:S(2)}) %copy-start) | copy-done | bytes 1572888
  1.4 94.2 %shard_map.37 = f32[384,1024]{1,0:T(8,128)S(1)} custom-call(bf16[3072,256]{1,0:T(8,128)(2,1)S(1)} %copy-done, bf16[1024,1024]{1,0:T(8,128)(2,1)} %b_ref.1, f32[384,1024]{1,0:T(8,128)} %r_ref.1), custom_call_target="tpu_custom_call" | custom-call | flops 6442450944 | bytes 3145728 | tf_op jit(solution)/shard_map/pallas_call | solution.py:296
  95.6 1.1 %copy.5 = f32[384,1024]{1,0:T(8,128)} copy(f32[384,1024]{1,0:T(8,128)S(1)} %shard_map.37) | data formatting | bytes 3145728
Async XLA Ops:
  0.0 1.4 %copy-start = (bf16[3072,256]{1,0:T(8,128)(2,1)S(1)}, bf16[3072,256]{1,0:T(8,128)(2,1)}, u32[]{:S(2)}) copy-start(bf16[3072,256]{1,0:T(8,128)(2,1)} %a_ref.1) | copy-start | bytes 4718596

commit v8 on v7

--- a/solution.py
+++ b/solution.py
@@ -102,9 +102,10 @@
         return remote(send.at[d, n], dn.at[d, n], z_s.at[d, n], dn_r.at[d, n], below)
 
     residual = pltpu.make_async_copy(r_ref, o_ref, r_s)
-    def product(d, n):
+    def product(d, n, wide=1):
         left = jnp.concatenate([a_all[d, p] for p in range(8)], axis=1)
-        return jnp.dot(left, b_all[n], preferred_element_type=jnp.float32)
+        right = jnp.concatenate([b_all[n + k] for k in range(wide)], axis=1)
+        return jnp.dot(left, right, preferred_element_type=jnp.float32)
 
     for n in range(nc):
         b_local(n).start()
@@ -126,10 +127,8 @@
 
     pl.semaphore_wait(barrier, 3 + (z + nz - 1) // nz + (2 * nz - 2 - z) // nz)
 
-    queue = []
-    for e in range(nz - 1):
-        queue += [("a", e), ("b", e)]
-    queue += [("b", n) for n in range(nz - 1, nc - 2)] + [("a", nz - 1), ("b", nc - 2), ("b", nc - 1)]
+    queue = [("a", 0), ("b", 0), ("a", 1), ("b", 1), ("a", 2), ("b", 2), ("b", 3), ("b", 4), ("b", 5),
+             ("b", 6), ("a", 3), ("b", 7)]
 
     def start_y(k):
         if k < len(queue):
@@ -169,13 +168,9 @@
     start_own(1)
     residual.wait()
 
-    head = [(0, 0)]
-    for e in range(1, nz - 1):
-        head += [(i, e) for i in range(e)] + [(e, n) for n in range(e + 1)]
-    sends = (nz - 1) * nc
-
-    def own_product(n, carry):
-        o_ref[:, columns(n)] += product(z, n)
+    def own_product(q, carry):
+        both = pl.ds(pl.multiple_of(2 * q * tile, 2 * tile), 2 * tile)
+        o_ref[:, both] += product(z, 2 * q, 2)
         return carry
 
     def add_arrivals(n, carry):
@@ -191,53 +186,17 @@
 
         return carry
 
-    def step(t, carry):
-        i = (t - len(head)) % (nz - 1)
-        n = nz - 1 + (t - len(head)) // (nz - 1)
-        for k, (head_i, head_n) in enumerate(head):
-            i = jnp.where(t == k, head_i, i)
-            n = jnp.where(t == k, head_n, n)
-        d = order(i)
-
-        @pl.when(t == 0)
-        def _():
-            a_arrives(0)
-            b_arrives(0)
-            a_complete(0)
-
-        for e in range(1, nz - 1):
-            @pl.when(t == head.index((0, e)))
-            def _():
-                a_arrives(e)
-                b_arrives(e)
-
-            @pl.when(t == head.index((e, 0)))
-            def _():
-                a_complete(e)
-
-        for e in range(nz - 1, nc):
-            @pl.when(t == len(head) + (e - nz + 1) * (nz - 1))
-            def _():
-                if e == nc - 2:
-                    a_arrives(nz - 1)
-                if e == nc - 1:
-                    a_complete(nz - 1)
-                    lax.fori_loop(0, nc - 1, own_product, 0)
-                    lax.fori_loop(0, nc - 4, add_arrivals, 0)
-                b_arrives(e)
-
-        part[...] = product(d, n)
-
+    def pass_on(d, n, value):
         @pl.when(d > z)
         def _():
             @pl.when(z > 0)
             def _():
                 c_up(d, n).wait_recv()
-                encode(send, d, n, part[...] + decode(up, d, n, rows))
+                encode(send, d, n, value[...] + decode(up, d, n, rows))
 
             @pl.when(z == 0)
             def _():
-                encode(send, d, n, part[...])
+                encode(send, d, n, value[...])
 
             c_up(d, n).start()
 
@@ -246,20 +205,71 @@
             @pl.when(z < nz - 1)
             def _():
                 c_dn(d, n).wait_recv()
-                encode(send, d, n, part[...] + decode(dn, d, n, rows))
+                encode(send, d, n, value[...] + decode(dn, d, n, rows))
 
             @pl.when(z == nz - 1)
             def _():
-                encode(send, d, n, part[...])
+                encode(send, d, n, value[...])
 
             c_dn(d, n).start()
 
-        return carry
-
-    lax.fori_loop(0, sends, step, 0)
-
-    own_product(nc - 1, 0)
-    lax.fori_loop(nc - 4, nc, add_arrivals, 0)
+    def run(tiles, arrivals, wide):
+        def step(t, carry):
+            i, n = tiles[0]
+            for k, (tile_i, tile_n) in enumerate(tiles[1:], 1):
+                i = jnp.where(t == k, tile_i, i)
+                n = jnp.where(t == k, tile_n, n)
+            for k, arrive in arrivals.items():
+                pl.when(t == k)(arrive)
+            d = order(i)
+            if wide == 1:
+                part[0] = product(d, n)
+                pass_on(d, n, part.at[0])
+            else:
+                both = product(d, n, 2)
+                part[0] = both[:, :tile]
+                part[1] = both[:, tile:]
+
+                def half(h, carry):
+                    pass_on(d, n + h, part.at[h])
+                    return carry
+
+                lax.fori_loop(0, 2, half, 0)
+            return carry
+
+        lax.fori_loop(0, len(tiles), step, 0)
+
+    def first():
+        a_arrives(0)
+        b_arrives(0)
+        a_complete(0)
+
+    def second():
+        a_arrives(1)
+        b_arrives(1)
+
+    def third():
+        a_arrives(2)
+        b_arrives(2)
+        b_arrives(3)
+
+    def fourth():
+        b_arrives(4)
+        b_arrives(5)
+
+    def last():
+        a_arrives(3)
+        lax.fori_loop(0, 4, add_arrivals, 0)
+        b_arrives(7)
+
+    run([(0, 0), (0, 1), (1, 0), (1, 1)], {0: first, 1: second, 2: lambda: a_complete(1)}, 1)
+    run([(0, 2), (1, 2), (2, 0), (2, 2), (0, 4), (1, 4), (2, 4)],
+        {0: third, 2: lambda: a_complete(2), 4: fourth}, 2)
+    run([(0, 6), (1, 6), (2, 6), (0, 7), (1, 7), (2, 7)], {0: lambda: b_arrives(6), 3: last}, 1)
+
+    a_complete(3)
+    lax.fori_loop(0, nc // 2, own_product, 0)
+    lax.fori_loop(4, nc, add_arrivals, 0)
 
     def drain_a(i, carry):
         a_y(i).wait_send()
@@ -301,7 +311,7 @@
         scratch_shapes=[
             pltpu.VMEM((nz, 8, rows, amplitudes.shape[1]), jnp.bfloat16),
             pltpu.VMEM((nc, depth, tile), jnp.bfloat16),
-            pltpu.VMEM((rows, tile), jnp.float32),
+            pltpu.VMEM((2, rows, tile), jnp.float32),
             pltpu.VMEM((nz, nc, rows + SCALE_ROWS, tile), jnp.bfloat16),
             pltpu.VMEM((nz, nc, rows + SCALE_ROWS, tile), jnp.bfloat16),
             pltpu.VMEM((nz, nc, rows + SCALE_ROWS, tile), jnp.bfloat16),
@@ -313,7 +323,7 @@
             dma((nz, nc)), dma((nz, nc)), dma((nz, nc)),
         ],
         compiler_params=pltpu.CompilerParams(
-            collective_id=0, has_side_effects=True, vmem_limit_bytes=50 * 1024 * 1024),
+            collective_id=0, has_side_effects=True, vmem_limit_bytes=52 * 1024 * 1024),
         cost_estimate=pl.CostEstimate(
             flops=2 * nz * rows * depth * cols, bytes_accessed=8 * rows * cols, transcendentals=0),
     )(amplitudes, integrals, old_residual)
@@ -338,7 +348,7 @@
 
 
 def per_device(amplitudes, integrals, old_residual):
-    if amplitudes.shape[1] % 128 or lax.axis_size("narrow") != 4 or lax.axis_size("wide") > 8:
+    if amplitudes.shape[1] % 128 or lax.axis_size("narrow") != 4 or lax.axis_size("wide") != 8:
         return ladder_gathered(amplitudes, integrals, old_residual)
     return ladder_kernel(amplitudes, integrals, old_residual)
 

time: 96.9 us -> 96.4 us (level)
  local copies, waits for them, and re-layouts: 2.55 us -> 1.15 us
    unnamed x3 -> x1, local copies, waits for them, and re-layouts: 2.55 us -> 1.15 us
where the time goes in v8:
time: 96.4 us; the launch traced here: 96.2 us
  Pallas kernels  95.1 us (99%)
  local copies, waits for them, and re-layouts  1.15 us (1%)
    pallas_call x1, Pallas kernels, ladder_kernel(): pl.pallas_call(functools.partial(kernel, nz, nc), out_shape=jax.ShapeDtyp...  95.1 us

profile of v8, /device:TPU:0, one launch (start us, length us, event | category | flops | bytes accessed | tf_op | source)
XLA Modules:
  0.0 96.2 jit_solution(9325673438593602536)
XLA Ops:
  0.0 95.1 %shard_map.37 = f32[384,1024]{1,0:T(8,128)S(1)} custom-call(bf16[3072,256]{1,0:T(8,128)(2,1)} %a_ref.1, bf16[1024,1024]{1,0:T(8,128)(2,1)} %b_ref.1, f32[384,1024]{1,0:T(8,128)} %r_ref.1), custom_call_target="tpu_custom_call" | custom-call | flops 6442450944 | bytes 3145728 | tf_op jit(solution)/shard_map/pallas_call | solution.py:306
  95.1 1.1 %copy.5 = f32[384,1024]{1,0:T(8,128)} copy(f32[384,1024]{1,0:T(8,128)S(1)} %shard_map.37) | data formatting | bytes 3145728

commit v9 on v4

--- a/solution.py
+++ b/solution.py
@@ -141,7 +141,7 @@
         start_y(queue.index(("a", i)) + AHEAD)
         a_x(i, 1).start()
         a_c(i, 1).start()
-        start_own(i + 2)
+        start_own(i + 1)
 
     def b_arrives(n):
         b_local(n).wait()
@@ -160,7 +160,6 @@
     for k in range(AHEAD):
         start_y(k)
     start_own(0)
-    start_own(1)
     residual.wait()
 
     head = [(0, 0)]
@@ -233,9 +232,13 @@
 
     a_complete(nz - 1)
 
+    def own_product(q, carry):
+        both = pl.ds(pl.multiple_of(2 * q * tile, 2 * tile), 2 * tile)
+        right = jnp.concatenate([b_all[2 * q], b_all[2 * q + 1]], axis=1)
+        o_ref[:, both] += jnp.dot(a_all[z], right, preferred_element_type=jnp.float32)
+        return carry
+
     def finish(n, carry):
-        o_ref[:, columns(n)] += jnp.dot(a_all[z], b_all[n], preferred_element_type=jnp.float32)
-
         @pl.when(z > 0)
         def _():
             c_up(z, n).wait_recv()
@@ -248,6 +251,7 @@
 
         return carry
 
+    lax.fori_loop(0, nc // 2, own_product, 0)
     lax.fori_loop(0, nc, finish, 0)
 
     def drain_a(i, carry):
@@ -302,7 +306,7 @@
             dma((nz, nc)), dma((nz, nc)), dma((nz, nc)),
         ],
         compiler_params=pltpu.CompilerParams(
-            collective_id=0, has_side_effects=True, vmem_limit_bytes=50 * 1024 * 1024),
+            collective_id=0, has_side_effects=True, vmem_limit_bytes=52 * 1024 * 1024),
         cost_estimate=pl.CostEstimate(
             flops=2 * nz * rows * depth * cols, bytes_accessed=8 * rows * cols, transcendentals=0),
     )(amplitudes, integrals, old_residual)

time: 93 us -> 90.1 us (0.969); the launches traced: 91.3 us -> 90 us
  local copies, waits for them, and re-layouts: 2.55 us -> 1.15 us
    unnamed x3 -> x1, local copies, waits for them, and re-layouts: 2.55 us -> 1.15 us
where the time goes in v9:
time: 90.1 us; the launch traced here: 90 us
  Pallas kernels  88.8 us (99%)
  local copies, waits for them, and re-layouts  1.15 us (1%)
    pallas_call x1, Pallas kernels, ladder_kernel(): pl.pallas_call(functools.partial(kernel, nz, nc), out_shape=jax.ShapeDtyp...  88.8 us

profile of v9, /device:TPU:0, one launch (start us, length us, event | category | flops | bytes accessed | tf_op | source)
XLA Modules:
  0.0 90.0 jit_solution(9507224589780919822)
XLA Ops:
  0.0 88.8 %shard_map.37 = f32[384,1024]{1,0:T(8,128)S(1)} custom-call(bf16[3072,256]{1,0:T(8,128)(2,1)} %a_ref.1, bf16[1024,1024]{1,0:T(8,128)(2,1)} %b_ref.1, f32[384,1024]{1,0:T(8,128)} %r_ref.1), custom_call_target="tpu_custom_call" | custom-call | flops 6442450944 | bytes 3145728 | tf_op jit(solution)/shard_map/pallas_call | solution.py:289
  88.8 1.1 %copy.5 = f32[384,1024]{1,0:T(8,128)} copy(f32[384,1024]{1,0:T(8,128)S(1)} %shard_map.37) | data formatting | bytes 3145728

commit v10 on v9

--- a/solution.py
+++ b/solution.py
@@ -125,7 +125,7 @@
     queue = []
     for e in range(nz - 1):
         queue += [("a", e), ("b", e)]
-    queue += [("b", n) for n in range(nz - 1, nc - 1)] + [("a", nz - 1), ("b", nc - 1)]
+    queue += [("b", n) for n in range(nz - 1, nc)] + [("a", nz - 1)]
 
     def start_y(k):
         if k < len(queue):
@@ -194,8 +194,6 @@
         for e in range(nz - 1, nc):
             @pl.when(t == len(head) + (e - nz + 1) * (nz - 1))
             def _():
-                if e == nc - 1:
-                    a_arrives(nz - 1)
                 b_arrives(e)
 
         part[...] = jnp.dot(a_all[d], b_all[n], preferred_element_type=jnp.float32)
@@ -230,7 +228,7 @@
 
     lax.fori_loop(0, sends, step, 0)
 
-    a_complete(nz - 1)
+    a_arrives(nz - 1)
 
     def own_product(q, carry):
         both = pl.ds(pl.multiple_of(2 * q * tile, 2 * tile), 2 * tile)
@@ -251,8 +249,10 @@
 
         return carry
 
+    lax.fori_loop(0, nc - 2, finish, 0)
+    a_complete(nz - 1)
     lax.fori_loop(0, nc // 2, own_product, 0)
-    lax.fori_loop(0, nc, finish, 0)
+    lax.fori_loop(nc - 2, nc, finish, 0)
 
     def drain_a(i, carry):
         a_y(i).wait_send()

time: 90.1 us -> 94.5 us (1.049)
  the two profiles are of different devices: /device:TPU:0 before, /device:TPU:9 now
where the time goes in v10:
time: 94.5 us; the launch traced here: 94.4 us
  Pallas kernels  93.2 us (99%)
  local copies, waits for them, and re-layouts  1.15 us (1%)
    pallas_call x1, Pallas kernels, ladder_kernel(): pl.pallas_call(functools.partial(kernel, nz, nc), out_shape=jax.ShapeDtyp...  93.2 us

profile of v10, /device:TPU:9, one launch (start us, length us, event | category | flops | bytes accessed | tf_op | source)
XLA Modules:
  0.0 94.4 jit_solution(3854054845028324109)
XLA Ops:
  0.0 93.2 %shard_map.37 = f32[384,1024]{1,0:T(8,128)S(1)} custom-call(bf16[3072,256]{1,0:T(8,128)(2,1)} %a_ref.1, bf16[1024,1024]{1,0:T(8,128)(2,1)} %b_ref.1, f32[384,1024]{1,0:T(8,128)} %r_ref.1), custom_call_target="tpu_custom_call" | custom-call | flops 6442450944 | bytes 3145728 | tf_op jit(solution)/shard_map/pallas_call | solution.py:289
  93.2 1.1 %copy.5 = f32[384,1024]{1,0:T(8,128)} copy(f32[384,1024]{1,0:T(8,128)S(1)} %shard_map.37) | data formatting | bytes 3145728

commit v11 on v9

--- a/solution.py
+++ b/solution.py
@@ -122,10 +122,8 @@
 
     pl.semaphore_wait(barrier, 3 + (z + nz - 1) // nz + (2 * nz - 2 - z) // nz)
 
-    queue = []
-    for e in range(nz - 1):
-        queue += [("a", e), ("b", e)]
-    queue += [("b", n) for n in range(nz - 1, nc - 1)] + [("a", nz - 1), ("b", nc - 1)]
+    queue = [("a", 0), ("b", 0)] + [("a", e) for e in range(1, nz - 1)] + [("b", n) for n in range(1, nc - 1)]
+    queue += [("a", nz - 1), ("b", nc - 1)]
 
     def start_y(k):
         if k < len(queue):
@@ -162,17 +160,10 @@
     start_own(0)
     residual.wait()
 
-    head = [(0, 0)]
-    for e in range(1, nz - 1):
-        head += [(i, e) for i in range(e)] + [(e, n) for n in range(e + 1)]
     sends = (nz - 1) * nc
 
     def step(t, carry):
-        i = (t - len(head)) % (nz - 1)
-        n = nz - 1 + (t - len(head)) // (nz - 1)
-        for k, (head_i, head_n) in enumerate(head):
-            i = jnp.where(t == k, head_i, i)
-            n = jnp.where(t == k, head_n, n)
+        n, i = t // (nz - 1), t % (nz - 1)
         d = order(i)
 
         @pl.when(t == 0)
@@ -182,17 +173,15 @@
             a_complete(0)
 
         for e in range(1, nz - 1):
-            @pl.when(t == head.index((0, e)))
-            def _():
-                a_arrives(e)
-                b_arrives(e)
-
-            @pl.when(t == head.index((e, 0)))
-            def _():
+            @pl.when(t == e)
+            def _():
+                if e == 1:
+                    for later in range(1, nz - 1):
+                        a_arrives(later)
                 a_complete(e)
 
-        for e in range(nz - 1, nc):
-            @pl.when(t == len(head) + (e - nz + 1) * (nz - 1))
+        for e in range(1, nc):
+            @pl.when(t == e * (nz - 1))
             def _():
                 if e == nc - 1:
                     a_arrives(nz - 1)

time: 90.1 us -> 95.5 us (1.060)
  Pallas kernels: 88.8 us -> 94.2 us
    pallas_call x1, Pallas kernels: 88.8 us -> 94.2 us  [ladder_kernel(): pl.pallas_call(functools.partial(kernel, nz, nc), out_shape=jax.ShapeDtyp...]
where the time goes in v11:
time: 95.5 us; the launch traced here: 95.4 us
  Pallas kernels  94.2 us (99%)
  local copies, waits for them, and re-layouts  1.15 us (1%)
    pallas_call x1, Pallas kernels, ladder_kernel(): pl.pallas_call(functools.partial(kernel, nz, nc), out_shape=jax.ShapeDtyp...  94.2 us

profile of v11, /device:TPU:0, one launch (start us, length us, event | category | flops | bytes accessed | tf_op | source)
XLA Modules:
  0.0 95.4 jit_solution(4002052823338944811)
XLA Ops:
  0.0 94.2 %shard_map.37 = f32[384,1024]{1,0:T(8,128)S(1)} custom-call(bf16[3072,256]{1,0:T(8,128)(2,1)} %a_ref.1, bf16[1024,1024]{1,0:T(8,128)(2,1)} %b_ref.1, f32[384,1024]{1,0:T(8,128)} %r_ref.1), custom_call_target="tpu_custom_call" | custom-call | flops 6442450944 | bytes 3145728 | tf_op jit(solution)/shard_map/pallas_call | solution.py:278
  94.2 1.1 %copy.5 = f32[384,1024]{1,0:T(8,128)} copy(f32[384,1024]{1,0:T(8,128)S(1)} %shard_map.37) | data formatting | bytes 3145728

commit v12 on v9

--- a/solution.py
+++ b/solution.py
@@ -50,6 +50,8 @@
     own = z + (1 - high) * (nz - 1 - 2 * z)
 
     def order(i):
+        inner = (i + 2) // 3 * (1 - i // 3)
+        i = i + inner * (nz - 1 - own) * (3 - 2 * i)
         last = (i + 1) // nz
         k = last * own + (1 - last) * (i + (i + nz - own) // nz)
         return k + (1 - high) * (nz - 1 - 2 * k)
@@ -331,7 +333,7 @@
 
 
 def per_device(amplitudes, integrals, old_residual):
-    if amplitudes.shape[1] % 128 or lax.axis_size("narrow") != 4 or lax.axis_size("wide") > 8:
+    if amplitudes.shape[1] % 128 or lax.axis_size("narrow") != 4 or lax.axis_size("wide") != 8:
         return ladder_gathered(amplitudes, integrals, old_residual)
     return ladder_kernel(amplitudes, integrals, old_residual)
 

time: 90.1 us -> 95.2 us (1.057)
  the two profiles are of different devices: /device:TPU:0 before, /device:TPU:17 now
where the time goes in v12:
time: 95.2 us; the launch traced here: 95.1 us
  Pallas kernels  93.9 us (99%)
  local copies, waits for them, and re-layouts  1.15 us (1%)
    pallas_call x1, Pallas kernels, ladder_kernel(): pl.pallas_call(functools.partial(kernel, nz, nc), out_shape=jax.ShapeDtyp...  93.9 us

profile of v12, /device:TPU:17, one launch (start us, length us, event | category | flops | bytes accessed | tf_op | source)
XLA Modules:
  0.0 95.1 jit_solution(16408006622979196230)
XLA Ops:
  0.0 93.9 %shard_map.37 = f32[384,1024]{1,0:T(8,128)S(1)} custom-call(bf16[3072,256]{1,0:T(8,128)(2,1)} %a_ref.1, bf16[1024,1024]{1,0:T(8,128)(2,1)} %b_ref.1, f32[384,1024]{1,0:T(8,128)} %r_ref.1), custom_call_target="tpu_custom_call" | custom-call | flops 6442450944 | bytes 3145728 | tf_op jit(solution)/shard_map/pallas_call | solution.py:291
  94.0 1.1 %copy.5 = f32[384,1024]{1,0:T(8,128)} copy(f32[384,1024]{1,0:T(8,128)S(1)} %shard_map.37) | data formatting | bytes 3145728

commit v13 on v9

--- a/solution.py
+++ b/solution.py
@@ -10,7 +10,7 @@
 SCALE_ROWS = 16
 KEEP = 46000.0
 CHUNKS = 8
-AHEAD = 3
+AHEAD = 4
 MESH = pl.DeviceIdType.MESH
 
 

time: 90.1 us -> 90.1 us (level)
  no operation moved by 1% of the time
where the time goes in v13:
time: 90.1 us; the launch traced here: 90 us
  Pallas kernels  88.8 us (99%)
  local copies, waits for them, and re-layouts  1.15 us (1%)
    pallas_call x1, Pallas kernels, ladder_kernel(): pl.pallas_call(functools.partial(kernel, nz, nc), out_shape=jax.ShapeDtyp...  88.8 us

profile of v13, /device:TPU:0, one launch (start us, length us, event | category | flops | bytes accessed | tf_op | source)
XLA Modules:
  0.0 90.0 jit_solution(6665621030337473891)
XLA Ops:
  0.0 88.8 %shard_map.37 = f32[384,1024]{1,0:T(8,128)S(1)} custom-call(bf16[3072,256]{1,0:T(8,128)(2,1)} %a_ref.1, bf16[1024,1024]{1,0:T(8,128)(2,1)} %b_ref.1, f32[384,1024]{1,0:T(8,128)} %r_ref.1), custom_call_target="tpu_custom_call" | custom-call | flops 6442450944 | bytes 3145728 | tf_op jit(solution)/shard_map/pallas_call | solution.py:289
  88.8 1.1 %copy.5 = f32[384,1024]{1,0:T(8,128)} copy(f32[384,1024]{1,0:T(8,128)S(1)} %shard_map.37) | data formatting | bytes 3145728
